TPU v7x, 512 devices: a whole 4x8x8 slice. The times are simulated.
512 devices in a mesh: img: 8 (over z_hi, x), patch: 64 (over z_lo, y, core).
Axes of the slice: x: 4, y: 8, z: 8 (z_hi: 2, z_lo: 4; z = z_hi * 4 + z_lo), core: 2. Of those that a mesh axis runs over, the one named last changes fastest.
Arguments:
- hidden_in: bfloat16 [16, 3072, 1280], P('img', 'patch'), parts along dimension 0, may hold values from -25 to 25
- gn_gain: float32 [1280], replicated, may hold values from 0.1 to 1.9
- gn_bias: float32 [1280], replicated, may hold values from -3 to 3
- stale_local: float32 [16, 64, 2, 32], P('img', 'patch'), parts along dimension 0, may hold values from -9600 to 480000, as said below
- w_qkv: bfloat16 [1280, 1920], P('patch'), may hold values from -0.15625 to 0.15625
- stale_values: bfloat16 [16, 3072, 1280], P('img', 'patch'), parts along dimension 0, may hold values from -1 to 1
- stale_scales: bfloat16 [16, 3072, 2], P('img', 'patch'), parts along dimension 0, may hold values from 1 to 200
Outputs:
- attended: bfloat16 [16, 3072, 640], P('img', 'patch'), parts along dimension 0
- fresh_values: bfloat16 [16, 3072, 1280], P('img', 'patch'), parts along dimension 0
- fresh_scales: bfloat16 [16, 3072, 2], P('img', 'patch'), parts along dimension 0
- gn_totals: float32 [16, 2, 32], P('img'), parts along dimension 0
There are 8 independent parts, one for each index of `img`. A program takes and returns all parts, laid end to end along the dimension named above; an argument that names none is the same for every part. Nothing has to cross between parts.
Inputs may be any that keep to these rules, and one draw needn't show every extreme that they name: stale_local[b, p, 1] is positive.
All inputs are finite; a program needn't handle non-finite values. Where the computation divides by a largest or mean magnitude, that divisor is 1e-20 or more.
Results may differ from a plain program's by a relative error of at most 0.0075.
The roundings to bfloat16 on the way count: a program that leaves them out, or rounds other values in their place, can miss the bound.
Values may be sent and summed in bfloat16 or wider, within the bound.
A program may use at most 128 MiB of HBM per device.

v0:
```python
import jax
import jax.numpy as jnp
from jax import lax
from jax.sharding import PartitionSpec as P

HEADS = 10
HEAD_DIM = 64
GROUPS = 32


def quantize(block):
    magnitude = jnp.max(jnp.abs(block.astype(jnp.float32)), axis=-1) + 1e-06
    codes = (block.astype(jnp.float32) / magnitude[..., None]).astype(jnp.bfloat16)
    return (codes, magnitude)


def local(hidden_in, gn_gain, gn_bias, stale_local, w_qkv, stale_values, stale_scales):
    images, tok_rows, model_width = hidden_in.shape
    patches = lax.axis_size("patch")
    own_index = lax.axis_index("patch")
    per_group = model_width // GROUPS
    head_cols = HEADS * HEAD_DIM
    features = hidden_in.astype(jnp.float32).reshape(images, tok_rows, GROUPS, per_group)
    fresh_sums = jnp.stack(
        [jnp.sum(features, axis=(1, 3)), jnp.sum(features * features, axis=(1, 3))], axis=1
    )
    stale_own = stale_local[:, 0]
    stale_all = lax.psum(stale_own, "patch")
    gn_totals = lax.psum(fresh_sums, "patch")
    used_sums = stale_all - stale_own + fresh_sums
    cell_count = float(tok_rows * patches * per_group)
    group_mean = used_sums[:, 0] / cell_count
    group_var = used_sums[:, 1] / cell_count - group_mean * group_mean
    normed = (features - group_mean[:, None, :, None]) * lax.rsqrt(group_var + 1e-05)[
        :, None, :, None
    ]
    normed = (normed.reshape(images, tok_rows, model_width) * gn_gain + gn_bias).astype(
        jnp.bfloat16
    )
    normed_flat = normed.reshape(images * tok_rows, model_width)
    projected = jnp.dot(
        normed_flat,
        lax.all_gather(w_qkv, "patch", axis=0, tiled=True),
        preferred_element_type=jnp.float32,
    ).astype(jnp.bfloat16)
    projected = projected.reshape(images, tok_rows, 3 * head_cols)
    queries = projected[:, :, :head_cols].reshape(images, tok_rows, HEADS, HEAD_DIM)
    fresh_keys = projected[:, :, head_cols : 2 * head_cols]
    fresh_vals = projected[:, :, 2 * head_cols :]
    key_codes, key_scale = quantize(fresh_keys)
    value_codes, value_scale = quantize(fresh_vals)
    fresh_values = jnp.concatenate([key_codes, value_codes], axis=2)
    fresh_scales = jnp.stack([key_scale, value_scale], axis=2).astype(jnp.bfloat16)
    own_keys = fresh_keys.reshape(images, tok_rows, HEADS, HEAD_DIM)
    own_vals = fresh_vals.reshape(images, tok_rows, HEADS, HEAD_DIM)
    own_scores = (
        jnp.einsum("bqhd,bkhd->bhqk", queries, own_keys, preferred_element_type=jnp.float32) * 0.125
    )
    top_own = jnp.max(own_scores, axis=3)
    own_lifted = jnp.exp(own_scores - top_own[..., None])
    running_sum = jnp.sum(own_lifted, axis=3)
    running_acc = jnp.einsum(
        "bhqk,bkhd->bhqd",
        own_lifted.astype(jnp.bfloat16),
        own_vals,
        preferred_element_type=jnp.float32,
    )
    codes = lax.all_gather(stale_values, "patch", axis=1, tiled=True)
    factors = lax.all_gather(stale_scales, "patch", axis=1, tiled=True)
    key_count = codes.shape[1]
    factors = factors.astype(jnp.float32)
    keys = codes[:, :, :head_cols].reshape(images, key_count, HEADS, HEAD_DIM)
    scores = (
        jnp.einsum("bqhd,bkhd->bkhq", queries, keys, preferred_element_type=jnp.float32)
        * factors[:, :, 0][:, :, None, None]
        * 0.125
    )
    positions = jnp.arange(key_count, dtype=jnp.int32)
    scores = jnp.where((positions // tok_rows == own_index)[None, :, None, None], -jnp.inf, scores)
    new_max = jnp.maximum(top_own, jnp.transpose(jnp.max(scores, axis=1), (0, 1, 2)))
    lifted = jnp.exp(scores - new_max[:, None])
    decay_factor = jnp.exp(top_own - new_max)
    weights = (lifted * factors[:, :, 1][:, :, None, None]).astype(jnp.bfloat16)
    values = codes[:, :, head_cols:].reshape(images, key_count, HEADS, HEAD_DIM)
    new_sum = running_sum * decay_factor + jnp.sum(lifted, axis=1)
    new_acc = running_acc * decay_factor[..., None] + jnp.einsum(
        "bkhq,bkhd->bhqd", weights, values, preferred_element_type=jnp.float32
    )
    mixed = new_acc / new_sum[..., None]
    attended = (
        jnp.transpose(mixed, (0, 2, 1, 3)).reshape(images, tok_rows, head_cols).astype(jnp.bfloat16)
    )
    return (attended, fresh_values, fresh_scales, gn_totals)


def solution(mesh):
    in_specs = (
        P("img", "patch", None),
        P(),
        P(),
        P("img", "patch", None, None),
        P("patch", None),
        P("img", "patch", None),
        P("img", "patch", None),
    )
    out_specs = (
        P("img", "patch", None),
        P("img", "patch", None),
        P("img", "patch", None),
        P("img", None, None),
    )
    return jax.shard_map(local, mesh=mesh, in_specs=in_specs, out_specs=out_specs, check_vma=False)
```

profile of v0, /device:TPU:1, one launch (start us, length us, event | category | flops | bytes accessed | tf_op | source)
XLA Modules:
  0.0 336.0 jit_solution(3773745156871774721)
XLA Ops:
  7.3 0.7 all-gather.6.cloned.1.call-update
  8.0 0.7 all-gather.4.cloned.1.call-update
  8.7 0.8 copy.50
  9.5 89.6 %all_gather.11 = bf16[2,3072,2]{2,0,1:T(2,128)(2,1)S(1)} all-gather(bf16[2,48,2]{2,0,1:T(2,128)(2,1)S(1)} %copy.50), channel_id=1, replica_groups=mesh['img'=8,'patch'=64] {'patch'}, dimensions={1}, use_global_device_ids=true | all-gather | bytes 24960 | tf_op jit(solution)/shard_map/all_gather | solution.py:69
  99.1 3.8 %fusion.36 = (f32[2,3072,1]{2,0,1:T(2,128)}, f32[2,3072,1]{2,0,1:T(2,128)S(1)}) fusion(bf16[2,3072,2]{2,0,1:T(2,128)(2,1)S(1)} %all_gather.11), kind=kLoop, calls=%fused_computation.67 | loop fusion | bytes 98304 | tf_op jit(solution)/shard_map/slice | solution.py:75
  102.9 3.9 %copy.51 = f32[2,3072,1]{1,0,2:T(2,128)S(1)} copy(f32[2,3072,1]{2,0,1:T(2,128)} %get-tuple-element.30) | data formatting | bytes 49152 | tf_op jit(solution)/shard_map/slice | solution.py:75
  107.3 136.2 %all-reduce = (f32[2,2,32]{2,1,0:T(2,128)S(1)}, f32[2,2,32]{2,1,0:T(2,128)}) all-reduce(f32[2,2,32]{2,1,0:T(2,128)S(1)} %bitcast.78, f32[2,2,32]{2,1,0:T(2,128)S(1)} %pad_maximum_fusion.1), channel_id=1, replica_groups=mesh['img'=8,'patch'=64] {'patch'}, use_global_device_ids=true, to_apply=%region_0.0 | all-reduce | flops 256 | bytes 2048 | tf_op jit(solution)/shard_map/psum | solution.py:28
  243.9 2.5 copy.52
  246.6 7.6 %reshape.127 = bf16[1280,1920]{1,0:T(8,128)(2,1)} reshape(bf16[64,20,1920]{2,1,0:T(8,128)(2,1)} %all-gather.6.cloned.1.call-done) | data formatting | bytes 9830400
  254.1 3.4 %convolution_convert_fusion = bf16[96,1920]{1,0:T(8,128)(2,1)S(1)} fusion(bf16[96,1280]{1,0:T(8,128)(2,1)S(1)} %bitcast.66, bf16[1280,1920]{1,0:T(8,128)(2,1)} %reshape.127), kind=kOutput, calls=%fused_computation.8 | convolution fusion | flops 472043520 | bytes 5529600 | tf_op jit(solution)/shard_map/dot_general | solution.py:41
  258.0 0.2 reshape.123
  258.4 0.6 copy.55
  259.0 0.3 fusion.38
  259.5 0.7 pad_maximum_fusion
  260.2 13.4 %all-gather.4.cloned.1.call-done = bf16[2,3072,1280]{2,1,0:T(8,128)(2,1)} async-done(((bf16[2,48,1280]{2,1,0:T(8,128)(2,1)}), bf16[2,3072,1280]{2,1,0:T(8,128)(2,1)}) %all-gather.4.cloned.1.call-update) | async-done | bytes 15728656 | tf_op jit(solution)/shard_map/all_gather | solution.py:68
  273.7 11.0 %fusion.35 = (bf16[2,3072,640]{2,1,0:T(8,128)(2,1)}, bf16[2,3072,640]{2,1,0:T(8,128)(2,1)}) fusion(bf16[2,3072,1280]{2,1,0:T(8,128)(2,1)} %all-gather.4.cloned.1.call-done), kind=kLoop, calls=%fused_computation.66 | loop fusion | bytes 31457280 | tf_op jit(solution)/shard_map/slice | solution.py:72
  284.7 10.6 %copy.53 = bf16[2,3072,640]{1,2,0:T(8,128)(2,1)} copy(bf16[2,3072,640]{2,1,0:T(8,128)(2,1)} %get-tuple-element.29) | data formatting | bytes 15728640 | tf_op jit(solution)/shard_map/slice | solution.py:84
  295.3 10.7 %copy.48 = bf16[2,3072,640]{1,2,0:T(8,128)(2,1)} copy(bf16[2,3072,640]{2,1,0:T(8,128)(2,1)} %get-tuple-element.28) | data formatting | bytes 15728640 | tf_op jit(solution)/shard_map/slice | solution.py:72
  305.9 4.7 %bitcast_reduce_fusion = (f32[2,10,48]{2,1,0:T(8,128)S(1)}, f32[2,10,48,3072]{3,2,1,0:T(8,128)S(1)}) fusion(f32[2,3072]{1,0:T(2,128)S(1)} %bitcast.67, pred[3072]{0:T(1024)(128)(4,1)S(1)} %fusion.28, bf16[2,3072,10,64]{1,3,2,0:T(8,128)(2,1)} %bitcast.61, bf16[2,48,10,64]{3,2,1,0:T(8,128)(2,1)S(1)} %reshape.121), kind=kOutput, calls=%fused_computation.1 | convolution fusion | flops 389282880 | bytes 19815168 | tf_op jit(solution)/shard_map/bqhd,bkhd->bkhq/dot_general | solution.py:74
  310.7 4.3 %copy-done = f32[2,10,48,3072]{3,2,1,0:T(8,128)} copy-done((f32[2,10,48,3072]{3,2,1,0:T(8,128)}, f32[2,10,48,3072]{3,2,1,0:T(8,128)S(1)}, u32[]{:S(2)}) %copy-start) | copy-done | bytes 11796504
  315.0 3.1 fusion.1
  318.1 9.6 %fusion.7 = f32[2,48,10,64]{3,1,2,0:T(8,128)S(1)} fusion(bf16[2,3072,10,64]{1,3,2,0:T(8,128)(2,1)} %bitcast.62, f32[2,10,48,3072]{3,2,1,0:T(8,128)} %copy-done, f32[2,3072]{1,0:T(2,128)S(1)} %bitcast.71, f32[2,10,48]{2,1,0:T(8,128)S(1)} %max.19, f32[2,3072]{1,0:T(2,128)S(1)} %bitcast.69, pred[3072]{0:T(1024)(128)(4,1)S(1)} %fusion.28), kind=kOutput, calls=%fused_computation.14 | convolution fusion | flops 395182080 | bytes 19962624 | tf_op jit(solution)/shard_map/bkhq,bkhd->bhqd/dot_general | solution.py:86
  327.7 0.5 fusion.8
  328.3 0.9 convert_element_type.46
  (38 shorter events, 2.0 us)
Async XLA Ops:
  7.2 99.6 %copy-start.1 = (bf16[2,48,1280]{2,1,0:T(8,128)(2,1)S(1)}, bf16[2,48,1280]{2,1,0:T(8,128)(2,1)}, u32[]{:S(2)}) copy-start(bf16[2,48,1280]{2,1,0:T(8,128)(2,1)} %param.7) | copy-start | bytes 737284
  7.2 100.1 %copy-start.4 = (f32[2,1,2,32]{3,2,1,0:T(2,128)S(1)}, f32[2,1,2,32]{3,2,1,0:T(2,128)}, u32[]{:S(2)}) copy-start(f32[2,1,2,32]{3,2,1,0:T(2,128)} %param.10) | copy-start | bytes 1540
  7.2 239.2 %copy-start.2 = (f32[1280]{0:T(1024)S(1)}, f32[1280]{0:T(1024)}, u32[]{:S(2)}) copy-start(f32[1280]{0:T(1024)} %param.9) | copy-start | bytes 15364
  7.2 239.2 %copy-start.3 = (f32[1280]{0:T(1024)S(1)}, f32[1280]{0:T(1024)}, u32[]{:S(2)}) copy-start(f32[1280]{0:T(1024)} %param.8) | copy-start | bytes 15364
  7.2 239.4 %all-gather.6.cloned.1.call-start = ((), (), s32[]{:S(2)}) async-start(), calls=%async_computation.1 | async-start | bytes 5990400 | tf_op jit(solution)/shard_map/all_gather | solution.py:43
  7.9 265.7 %all-gather.4.cloned.1.call-start = ((), (), s32[]{:S(2)}) async-start(), calls=%async_computation | async-start | bytes 15974400 | tf_op jit(solution)/shard_map/all_gather | solution.py:68
  310.6 4.4 %copy-start = (f32[2,10,48,3072]{3,2,1,0:T(8,128)}, f32[2,10,48,3072]{3,2,1,0:T(8,128)S(1)}, u32[]{:S(2)}) copy-start(f32[2,10,48,3072]{3,2,1,0:T(8,128)S(1)} %get-tuple-element.46) | copy-start | bytes 35389444
Sparse Core Ops, SparseCore 0:
  10.2 128.9 all-gather.5
  141.3 132.3 all-gather.3
where the time goes:
time: 337 us; the launch traced here: 336 us
  blocking collectives  226 us (67%)
  local copies, waits for them, and re-layouts  58.1 us (17%)
  matrix products  18.5 us (5%)
  waiting for transfers between devices  14.8 us (4%)
  between operations  14.3 us (4%)
  other arithmetic  4.6 us (1%)
    psum x1, blocking collectives, local(): stale_all = lax.psum(stale_own, 'patch')  136 us
    all_gather x1, blocking collectives, local(): factors = lax.all_gather(stale_scales, 'patch', axis=1, tiled=True)  89.6 us
    slice x2, local copies, waits for them, and re-layouts, local(): keys = codes[:, :, :head_cols].reshape(images, key_count, HEADS, HEAD_DIM)  21.7 us
    all_gather x1, waiting for transfers between devices, local(): codes = lax.all_gather(stale_values, 'patch', axis=1, tiled=True)  13.4 us
    unnamed x13, local copies, waits for them, and re-layouts  13.3 us
    slice x1, local copies, waits for them, and re-layouts, local(): values = codes[:, :, head_cols:].reshape(images, key_count, HEADS, HEAD_DIM)  10.6 us
    dot_general x1, matrix products, local(): jnp.einsum('bkhq,bkhd->bhqd', weights, values, preferred_element_type=jnp...  9.63 us
    slice x2, local copies, waits for them, and re-layouts, local(): factors[:, :, 0][:, :, None, None]  7.74 us
  transfers between devices with their start and end apart: 2, of which 1 were waited for; matrix products, arithmetic and copies ran while one was open for 8% of the time, Pallas kernels for 0%

commit v1 on v0

v1 whole, which is shorter than its diff:
```python
import jax
import jax.numpy as jnp
from jax import lax
from jax.experimental import pallas as pl
from jax.experimental.pallas import tpu as pltpu
from jax.sharding import PartitionSpec as P

HEADS = 10
HEAD_DIM = 64
GROUPS = 32
D = 1280
CPG = 40
ROWS = 48
NY = 8
NZ = 4
NX = 4
QROWS = NY * ROWS
UNITS = 3
CHUNK = UNITS * ROWS + 16
WCOLS = 640
CELLS = 122880.0
BIG_NEG = -1e30
OFF = (0, 1, -1, 2, -2, 3, -3, 4)
KV_GROUPS = ((0, 3), (3, 2), (5, 3))
MESH = pl.DeviceIdType.MESH
F32 = jnp.float32
BF16 = jnp.bfloat16


def head_of(group, unit):
    return min(UNITS * group + unit, HEADS - 1)


def lane_low(shape):
    return lax.broadcasted_iota(jnp.int32, shape, 1) < HEAD_DIM


def join_halves(low, low_high, high, high_high):
    left = pltpu.roll(low, HEAD_DIM, 1) if low_high else low
    right = high if high_high else pltpu.roll(high, HEAD_DIM, 1)
    return jnp.where(lane_low(left.shape), left, right)


def kernel(
    hid_ref,
    gain_ref,
    bias_ref,
    stale_ref,
    w_ref,
    codes_ref,
    scales_ref,
    att_ref,
    fvals_ref,
    fscales_ref,
    totals_ref,
    kvs,
    kv,
    kv2,
    kvf,
    xbuf,
    xn,
    st,
    stbuf,
    stsib,
    stz,
    w32,
    wpack,
    w0,
    w80,
    wbuf,
    qbuf,
    mask_diag,
    mask_off,
    m_ref,
    l_ref,
    acc_ref,
    fsend,
    fhome,
    asend,
    ahome,
    kvy_s,
    kvy_r,
    kvup_s,
    kvdn_s,
    kvz_r,
    kvsib_s,
    kvsib_r,
    x_s,
    x_r,
    sty_s,
    sty_r,
    stsib_s,
    stsib_r,
    stz_s,
    stz_r,
    p0_s,
    p0_r,
    wy_s,
    wy_r,
    wz_s,
    wz_r,
    wx_s,
    wx_r,
    ws_s,
    ws_r,
    f_s,
    f_r,
    a_s,
    a_r,
):
    img = lax.axis_index("img")
    patch = lax.axis_index("patch")
    x = img % NX
    img_base = img - x
    z = patch // (2 * NY)
    y = (patch // 2) % NY
    c = patch % 2

    def dev(y_at=None, z_at=None, c_at=None, x_at=None):
        yy = y if y_at is None else y_at
        zz = z if z_at is None else z_at
        cc = c if c_at is None else c_at
        xx = x if x_at is None else x_at
        return {"img": img_base + xx, "patch": (zz * NY + yy) * 2 + cc}

    sib = dev(c_at=1 - c)
    y_peers = [dev(y_at=(y + k) % NY) for k in range(1, NY)]
    z_peers = [dev(z_at=(z + k) % NZ) for k in range(1, NZ)]
    x_peers = [dev(x_at=(x + k) % NX) for k in range(1, NX)]
    y_twin = y + 1 - 2 * (y % 2)
    diag = dev(y_at=y_twin, c_at=1 - c)
    everyone = y_peers + z_peers + x_peers + [sib, diag]

    barrier = pltpu.get_barrier_semaphore()
    for peer in everyone:
        pl.semaphore_signal(barrier, inc=1, device_id=peer, device_id_type=MESH)

    img_b = y % 2
    active = (y // 2) == x
    four = (y % 2) * 2 + c
    w_core = c == (y // 2) % 2

    pending = []

    def send(src, dst, s_sem, r_sem, peer, when=None):
        copy = pltpu.make_async_remote_copy(
            src_ref=src, dst_ref=dst, send_sem=s_sem, recv_sem=r_sem, device_id=peer, device_id_type=MESH
        )

        def start():
            copy.start()

        def finish():
            copy.wait_send()

        if when is None:
            start()
            pending.append(finish)
        else:
            pl.when(when)(start)
            pending.append(lambda: pl.when(when)(finish))

    def received(dst, s_sem, r_sem):
        pltpu.make_async_remote_copy(
            src_ref=dst, dst_ref=dst, send_sem=s_sem, recv_sem=r_sem, device_id=sib, device_id_type=MESH
        ).wait_recv()

    @pl.when(active)
    def _():
        w32[...] = jnp.zeros_like(w32)
        w32[0:20, :] = w_ref[...].astype(F32)

        def piece(block, head):
            unit = block * HEADS + head
            return w32[:, (unit // 2) * 128 : (unit // 2) * 128 + 128], unit % 2 == 1

        for g in range(4):
            h = [head_of(g, s) for s in range(UNITS)]
            plan = [((1, h[s]), (2, h[s])) for s in range(UNITS)]
            plan += [((0, h[0]), (0, h[1])), ((0, h[2]), (0, h[2]))]
            for t, (first, second) in enumerate(plan):
                a, a_high = piece(*first)
                b, b_high = piece(*second)
                wpack[g, :, t * 128 : t * 128 + 128] = join_halves(a, a_high, b, b_high).astype(BF16)

    for b in range(2):
        lane16 = lax.broadcasted_iota(jnp.int32, (16, 128), 1)
        sc = scales_ref[b].astype(F32)
        tile = jnp.zeros((16, 128), F32)
        for t in range(3):
            for f in range(2):
                col = sc[t * 16 : t * 16 + 16, f : f + 1]
                tile = jnp.where(lane16 == 2 * t + f, col, tile)
        tile = tile.astype(BF16)
        packed = {}
        for h in range(HEADS):
            k_tile = codes_ref[b, :, (h // 2) * 128 : (h // 2) * 128 + 128].astype(F32)
            v_tile = codes_ref[b, :, 640 + (h // 2) * 128 : 640 + (h // 2) * 128 + 128].astype(F32)
            odd = h % 2 == 1
            packed[h] = join_halves(k_tile, odd, v_tile, odd).astype(BF16)
        for g in range(4):
            for s in range(UNITS):
                kvs[2 * g + b, s * ROWS : (s + 1) * ROWS, :] = packed[head_of(g, s)]
            kvs[2 * g + b, UNITS * ROWS : CHUNK, :] = tile

    sub = lax.broadcasted_iota(jnp.int32, (GROUPS, D), 0) * CPG
    lane = lax.broadcasted_iota(jnp.int32, (GROUPS, D), 1)
    spread = jnp.where((lane >= sub) & (lane < sub + CPG), 1.0, 0.0).astype(F32)
    col_sums = []
    for b in range(2):
        feats = hid_ref[b].astype(F32)
        col_sums.append(jnp.sum(feats, axis=0, keepdims=True))
        col_sums.append(jnp.sum(feats * feats, axis=0, keepdims=True))
    col_sums = jnp.concatenate(col_sums, axis=0)
    fresh = lax.dot_general(
        col_sums, spread, (((1,), (1,)), ((), ())), precision=lax.Precision.HIGHEST, preferred_element_type=F32
    )
    st[...] = jnp.zeros_like(st)
    st[0:4, 0:GROUPS] = stale_ref[...]
    st[4:8, 0:GROUPS] = fresh
    stbuf[y] = st[...]

    kv[z, c, 0] = kvs[y]
    xbuf[0] = hid_ref[img_b]

    pl.semaphore_wait(barrier, len(everyone))

    for j in range(4):
        peer = dev(y_at=y - y % 2 + j // 2, c_at=j % 2)
        send(wpack.at[j], w0.at[pl.ds(pl.multiple_of(four * 32, 32), 32)], p0_s.at[j], p0_r.at[four], peer, active & (four != j))
    for i in range(1, NY):
        send(kvs.at[(y - OFF[i]) % NY], kv.at[z, c, i], kvy_s.at[i], kvy_r.at[i], dev(y_at=(y - OFF[i]) % NY))
    for k in range(1, NY):
        send(st, stbuf.at[y], sty_s.at[k], sty_r.at[y], dev(y_at=(y + k) % NY))
    for i in range(1, NY):
        dest = (y - OFF[i]) % NY
        send(hid_ref.at[dest % 2], xbuf.at[i], x_s.at[i], x_r.at[i], dev(y_at=dest))

    for i in range(NY):
        lane_q = lax.broadcasted_iota(jnp.int32, (ROWS, QROWS), 1)
        same = (lane_q >= i * ROWS) & (lane_q < (i + 1) * ROWS)
        mask_diag[i * ROWS : (i + 1) * ROWS, :] = jnp.where(same, 0.0, BIG_NEG)
        mask_off[i * ROWS : (i + 1) * ROWS, :] = jnp.where(same, BIG_NEG, 0.0)

    w_rows = pl.ds(pl.multiple_of((z * 4 + x) * 80, 80), 80)
    for j in range(4):

        @pl.when(active & (four != j))
        def _(j=j):
            received(w0.at[pl.ds(j * 32, 32)], p0_s.at[j], p0_r.at[j])

    @pl.when(active)
    def _():
        w0[pl.ds(pl.multiple_of(four * 32, 32), 32), :] = wpack[four]
        row = lax.broadcasted_iota(jnp.int32, (80, 128), 0)
        col = lax.broadcasted_iota(jnp.int32, (80, 128), 1)
        hit = jnp.zeros((80, 128), F32)
        for a in range(4):
            hit = jnp.where((row >= 20 * a) & (row < 20 * a + 20) & (col == row + 12 * a), 1.0, hit)
        w80[...] = jnp.dot(hit.astype(BF16), w0[...], preferred_element_type=F32).astype(BF16)

    for k in range(2):
        plane = 2 * four + k

        @pl.when(active & (plane == y))
        def _():
            wbuf[w_rows, :] = w80[...]

        send(w80, wbuf.at[w_rows], wy_s.at[k], wy_r.at[0], dev(y_at=plane), active & (plane != y))

    def kv_part(zz, cc, grp):
        first, count = KV_GROUPS[grp]
        return kv.at[zz, cc, pl.ds(first, count)]

    def kv_forward(zz, grp, up, down):
        part = kv_part(zz, c, grp)
        if up is not None:
            send(part, part, kvup_s.at[zz, grp], kvz_r.at[zz, grp], dev(z_at=jnp.minimum(z + 1, NZ - 1)), up)
        if down is not None:
            send(part, part, kvdn_s.at[zz, grp], kvz_r.at[zz, grp], dev(z_at=jnp.maximum(z - 1, 0)), down)

    def kv_own(grp):
        first, count = KV_GROUPS[grp]
        for i in range(first, first + count):
            if i > 0:
                received(kv.at[z, c, i], kvy_s.at[i], kvy_r.at[i])
        kv_forward(z, grp, z < NZ - 1, z > 0)
        part = kv_part(z, c, grp)
        send(part, part, kvsib_s.at[z, grp], kvsib_r.at[z, grp], sib)

    def kv_relay(dist, grp):
        for sign in (-1, 1):
            src_z = z + sign * dist
            there = (src_z >= 0) & (src_z < NZ)
            zz = jnp.clip(src_z, 0, NZ - 1)
            part = kv_part(zz, c, grp)

            @pl.when(there)
            def _(part=part, zz=zz):
                received(part, kvup_s.at[zz, grp], kvz_r.at[zz, grp])

            if dist < NZ - 1:
                if sign < 0:
                    kv_forward(zz, grp, there & (z < NZ - 1), None)
                else:
                    kv_forward(zz, grp, None, there & (z > 0))
            send(part, part, kvsib_s.at[zz, grp], kvsib_r.at[zz, grp], sib, there)

    kv_own(0)
    kv_own(1)

    def w_block(zz, xx):
        return wbuf.at[pl.ds(pl.multiple_of((zz * 4 + xx) * 80, 80), 80)]

    @pl.when(w_core & jnp.logical_not(active & (y // 2 == four)))
    def _():
        received(w_block(z, x), wy_s.at[0], wy_r.at[0])

    for k in range(1, NZ):
        send(w_block(z, x), w_block(z, x), wz_s.at[k], wz_r.at[z], dev(z_at=(z + k) % NZ), w_core)

    def w_along_x(zz):
        for k in range(1, NX):
            send(w_block(zz, x), w_block(zz, x), wx_s.at[zz, k], wx_r.at[zz, x], dev(x_at=(x + k) % NX), w_core)

    w_along_x(z)
    kv_own(2)
    for k in range(1, NZ):
        zz = (z + k) % NZ

        @pl.when(w_core)
        def _(zz=zz):
            received(w_block(zz, x), wz_s.at[1], wz_r.at[zz])

        w_along_x(zz)

    for k in range(1, NY):
        yy = (y + k) % NY
        received(stbuf.at[yy], sty_s.at[k], sty_r.at[yy])
    y_sum = stbuf[0]
    for k in range(1, NY):
        y_sum = y_sum + stbuf[k]
    stsib[0] = y_sum
    send(stsib.at[0], stsib.at[1], stsib_s, stsib_r, sib)

    for grp in range(3):
        kv_relay(1, grp)

    received(stsib.at[1], stsib_s, stsib_r)
    stz[z] = stsib[0] + stsib[1]
    for k in range(1, NZ):
        send(stz.at[z], stz.at[z], stz_s.at[k], stz_r.at[z], dev(z_at=(z + k) % NZ))

    for grp in range(3):
        kv_relay(2, grp)

    def w_four(zz):
        return wbuf.at[pl.ds(pl.multiple_of(zz * 320, 320), 320)]

    for zz in range(NZ):
        for k in range(1, NX):
            xx = (x + k) % NX

            @pl.when(w_core)
            def _(zz=zz, xx=xx):
                received(w_block(zz, xx), wx_s.at[zz, 1], wx_r.at[zz, xx])

        send(w_four(zz), w_four(zz), ws_s.at[zz], ws_r.at[zz], sib, w_core)

    for grp in range(3):
        kv_relay(3, grp)

    for k in range(1, NZ):
        zz = (z + k) % NZ
        received(stz.at[zz], stz_s.at[k], stz_r.at[zz])
    total = stz[0]
    for k in range(1, NZ):
        total = total + stz[k]
    totals_ref[...] = total[4:8, 0:GROUPS]
    stat_rows = []
    for i in range(NY):
        own = stbuf[(y + OFF[i]) % NY]
        used = total[0:4, 0:GROUPS] - own[0:4, 0:GROUPS] + own[4:8, 0:GROUPS]
        used = jnp.where(img_b == 0, used[0:2], used[2:4])
        mean = used[0:1] / CELLS
        var = used[1:2] / CELLS - mean * mean
        stat_rows += [mean, lax.rsqrt(var + 1e-5)]
    stats = lax.dot_general(
        jnp.concatenate(stat_rows, axis=0),
        spread,
        (((1,), (0,)), ((), ())),
        precision=lax.Precision.HIGHEST,
        preferred_element_type=F32,
    )
    for i in range(NY):
        if i > 0:
            received(xbuf.at[i], x_s.at[i], x_r.at[i])
        feats = xbuf[i].astype(F32)
        normed = (feats - stats[2 * i : 2 * i + 1]) * stats[2 * i + 1 : 2 * i + 2]
        xn[i * ROWS : (i + 1) * ROWS, :] = (normed * gain_ref[...] + bias_ref[...]).astype(BF16)

    for zz in range(NZ):

        @pl.when(jnp.logical_not(w_core))
        def _(zz=zz):
            received(w_four(zz), ws_s.at[zz], ws_r.at[zz])

    fsend[...] = jnp.dot(xn[...], wbuf[:, 0:384], preferred_element_type=F32).astype(BF16).reshape(NY, ROWS, 384)
    for i in range(1, NY):
        home = (y + OFF[i]) % NY
        send(fsend.at[i], fhome.at[y], f_s.at[i], f_r.at[y], dev(y_at=home))
    fhome[y] = fsend[0]
    q_all = jnp.dot(xn[...], wbuf[:, 384:640], preferred_element_type=F32).astype(BF16).astype(F32) * 0.125
    low = lane_low((QROWS, 128))
    for s in range(UNITS):
        part = q_all[:, 0:128] if s < 2 else q_all[:, 128:256]
        if s == 1:
            part = pltpu.roll(part, HEAD_DIM, 1)
        part = jnp.where(low, part, 0.0).astype(BF16)
        qbuf[s, :, 0:128] = part
        qbuf[s, :, 128:256] = part
        kvf[s, :, 0:128] = fsend[:, :, s * 128 : s * 128 + 128].reshape(QROWS, 128)
        kvf[s, :, 128:256] = jnp.zeros((QROWS, 128), BF16)

    for zz in range(NZ):
        for grp in range(3):
            received(kv_part(zz, 1 - c, grp), kvsib_s.at[zz, grp], kvsib_r.at[zz, grp])

    low16 = lane_low((16, 128))

    def widen(step, carry):
        zc = step // NY
        slot = step % NY
        scale_tile = kv[zc // 2, zc % 2, slot, UNITS * ROWS : CHUNK, :].astype(F32)
        for t in range(3):
            factor = jnp.where(low16, scale_tile[:, 2 * t : 2 * t + 1], scale_tile[:, 2 * t + 1 : 2 * t + 2])
            for s in range(UNITS):
                code = kv[zc // 2, zc % 2, slot, s * ROWS + t * 16 : s * ROWS + t * 16 + 16, :].astype(F32)
                wide = code * factor
                high = wide.astype(BF16)
                rest = (wide - high.astype(F32)).astype(BF16)
                at = pl.ds(pl.multiple_of(slot * ROWS + t * 16, 16), 16)
                kv2[s, zc, at, 0:128] = high
                kv2[s, zc, at, 128:256] = rest
        return carry

    lax.fori_loop(0, 8 * NY, widen, 0)

    def attend(s, block, mask, first):
        scores = lax.dot_general(qbuf[s], block, (((1,), (1,)), ((), ())), preferred_element_type=F32)
        if mask is not None:
            scores = scores + mask
        top = jnp.max(scores, axis=1, keepdims=True)
        if first:
            new = jnp.broadcast_to(top, (QROWS, 128))
        else:
            old = m_ref[s]
            new = jnp.maximum(old, top)
            decay = jnp.exp(old - new)
        lifted = jnp.exp(scores - jnp.concatenate([new] * 3, axis=1))
        row_sum = lifted[:, 0:128] + lifted[:, 128:256] + lifted[:, 256:384]
        mixed = jnp.dot(lifted.astype(BF16), block, preferred_element_type=F32)
        m_ref[s] = new
        if first:
            l_ref[s] = row_sum
            acc_ref[s] = mixed
        else:
            l_ref[s] = l_ref[s] * decay + row_sum
            acc_ref[s] = acc_ref[s] * jnp.concatenate([decay, decay], axis=1) + mixed

    own_zc = z * 2 + c
    for s in range(UNITS):
        attend(s, kvf[s], mask_diag[...], True)
    for s in range(UNITS):
        attend(s, kv2[s, own_zc], mask_off[...], False)

    def others(k, carry):
        zc = (own_zc + k) % 8
        for s in range(UNITS):
            attend(s, kv2[s, zc], None, False)
        return carry

    lax.fori_loop(1, 8, others, 0)

    out = []
    for s in range(UNITS):
        total_l = jnp.sum(l_ref[s], axis=1, keepdims=True)
        out.append((acc_ref[s, :, 0:128] + acc_ref[s, :, 128:256]) / total_l)
    asend[:, :, 0:128] = join_halves(out[0], True, out[1], True).astype(BF16).reshape(NY, ROWS, 128)
    asend[:, :, 128:256] = out[2].astype(BF16).reshape(NY, ROWS, 128)
    for i in range(1, NY):
        home = (y + OFF[i]) % NY
        send(asend.at[i], ahome.at[y], a_s.at[i], a_r.at[y], dev(y_at=home))
    ahome[y] = asend[0]

    for k in range(1, NY):
        plane = (y + k) % NY
        received(fhome.at[plane], f_s.at[k], f_r.at[plane])
    for b in range(2):
        blocks = []
        for h in range(HEADS):
            g, s = (h // UNITS, h % UNITS)
            blocks.append(fhome[2 * g + b, :, s * 128 : s * 128 + 128].astype(F32))
        magnitudes = []
        for kind in range(2):
            tiles = [join_halves(blocks[2 * m], kind == 1, blocks[2 * m + 1], kind == 1) for m in range(5)]
            top = jnp.abs(tiles[0])
            for tile in tiles[1:]:
                top = jnp.maximum(top, jnp.abs(tile))
            magnitude = jnp.max(top, axis=1, keepdims=True) + 1e-06
            magnitudes.append(magnitude)
            for m in range(5):
                at = kind * 640 + m * 128
                fvals_ref[b, :, at : at + 128] = (tiles[m] / magnitude).astype(BF16)
        fscales_ref[b] = jnp.concatenate(magnitudes, axis=1).astype(BF16)

    for k in range(1, NY):
        plane = (y + k) % NY
        received(ahome.at[plane], a_s.at[k], a_r.at[plane])
    for b in range(2):
        pairs = [ahome[2 * g + b, :, 0:128].astype(F32) for g in range(4)]
        lasts = [ahome[2 * g + b, :, 128:256].astype(F32) for g in range(4)]
        att_ref[b, :, 0:128] = pairs[0].astype(BF16)
        att_ref[b, :, 128:256] = join_halves(lasts[0], True, pairs[1], False).astype(BF16)
        att_ref[b, :, 256:384] = join_halves(pairs[1], True, lasts[1], True).astype(BF16)
        att_ref[b, :, 384:512] = pairs[2].astype(BF16)
        att_ref[b, :, 512:640] = join_halves(lasts[2], True, pairs[3], False).astype(BF16)

    for finish in pending:
        finish()


def local(hidden_in, gn_gain, gn_bias, stale_local, w_qkv, stale_values, stale_scales):
    dma = pltpu.SemaphoreType.DMA
    vmem = pltpu.VMEM
    scratch = [
        vmem((NY, CHUNK, 128), BF16),
        vmem((NZ, 2, NY, CHUNK, 128), BF16),
        vmem((UNITS, 8, QROWS, 256), BF16),
        vmem((UNITS, QROWS, 256), BF16),
        vmem((NY, ROWS, D), BF16),
        vmem((QROWS, D), BF16),
        vmem((8, 128), F32),
        vmem((NY, 8, 128), F32),
        vmem((2, 8, 128), F32),
        vmem((NZ, 8, 128), F32),
        vmem((32, 1920), F32),
        vmem((4, 32, WCOLS), BF16),
        vmem((128, WCOLS), BF16),
        vmem((80, WCOLS), BF16),
        vmem((D, WCOLS), BF16),
        vmem((UNITS, QROWS, 256), BF16),
        vmem((QROWS, QROWS), F32),
        vmem((QROWS, QROWS), F32),
        vmem((UNITS, QROWS, 128), F32),
        vmem((UNITS, QROWS, 128), F32),
        vmem((UNITS, QROWS, 256), F32),
        vmem((NY, ROWS, 384), BF16),
        vmem((NY, ROWS, 384), BF16),
        vmem((NY, ROWS, 256), BF16),
        vmem((NY, ROWS, 256), BF16),
        dma((NY,)),
        dma((NY,)),
        dma((NZ, 3)),
        dma((NZ, 3)),
        dma((NZ, 3)),
        dma((NZ, 3)),
        dma((NZ, 3)),
        dma((NY,)),
        dma((NY,)),
        dma((NY,)),
        dma((NY,)),
        dma(()),
        dma(()),
        dma((NZ,)),
        dma((NZ,)),
        dma((4,)),
        dma((4,)),
        dma((2,)),
        dma((1,)),
        dma((NZ,)),
        dma((NZ,)),
        dma((NZ, NX)),
        dma((NZ, NX)),
        dma((NZ,)),
        dma((NZ,)),
        dma((NY,)),
        dma((NY,)),
        dma((NY,)),
        dma((NY,)),
    ]
    whole = pl.BlockSpec(memory_space=pltpu.VMEM)
    attended, fresh_values, fresh_scales, totals = pl.pallas_call(
        kernel,
        out_shape=(
            jax.ShapeDtypeStruct((2, ROWS, 640), BF16),
            jax.ShapeDtypeStruct((2, ROWS, D), BF16),
            jax.ShapeDtypeStruct((2, ROWS, 2), BF16),
            jax.ShapeDtypeStruct((4, GROUPS), F32),
        ),
        in_specs=[whole] * 7,
        out_specs=(whole,) * 4,
        scratch_shapes=scratch,
        compiler_params=pltpu.CompilerParams(
            collective_id=0, has_side_effects=True, vmem_limit_bytes=48 * 2**20
        ),
        name="attend_planes",
    )(
        hidden_in,
        gn_gain.reshape(1, D),
        gn_bias.reshape(1, D),
        stale_local.reshape(4, GROUPS),
        w_qkv,
        stale_values,
        stale_scales,
    )
    return attended, fresh_values, fresh_scales, totals.reshape(2, 2, GROUPS)


def solution(mesh):
    in_specs = (
        P("img", "patch", None),
        P(),
        P(),
        P("img", "patch", None, None),
        P("patch", None),
        P("img", "patch", None),
        P("img", "patch", None),
    )
    out_specs = (
        P("img", "patch", None),
        P("img", "patch", None),
        P("img", "patch", None),
        P("img", None, None),
    )
    return jax.shard_map(local, mesh=mesh, in_specs=in_specs, out_specs=out_specs, check_vma=False)
```

time: 337 us -> 102 us (0.30)
  blocking collectives: 226 us -> 0 us
  Pallas kernels: 0 us -> 92.9 us
  local copies, waits for them, and re-layouts: 58.1 us -> 7.41 us
  matrix products: 18.5 us -> 0 us
  waiting for transfers between devices: 14.8 us -> 0 us
  between operations: 14.3 us -> 0.67 us
  other arithmetic: 4.6 us -> 0 us
    psum x1 -> x0, blocking collectives: 136 us -> none  [local(): stale_all = lax.psum(stale_own, 'patch')]
    pallas_call x0 -> x1, Pallas kernels: none -> 92.9 us  [local(): pl.pallas_call(kernel, out_shape=(jax.ShapeDtypeStruct((2, ROWS, 640), BF...]
    all_gather x1 -> x0, blocking collectives: 89.6 us -> none  [local(): factors = lax.all_gather(stale_scales, 'patch', axis=1, tiled=True)]
    slice x7 -> x0, local copies, waits for them, and re-layouts: 42.6 us -> none  [the longest x2 21.7 us: local(): keys = codes[:, :, :head_cols].reshape(images, key_count, HEADS, HEAD_DIM)]
    dot_general x5 -> x0, matrix products: 18.5 us -> none  [the longest x1 9.63 us: local(): jnp.einsum('bkhq,bkhd->bhqd', weights, values, preferred_element_type=jnp...]
    all_gather x2 -> x0, waiting for transfers between devices: 13.4 us -> none  [the longest x1 13.4 us: local(): codes = lax.all_gather(stale_values, 'patch', axis=1, tiled=True)]
    unnamed x13 -> x17, local copies, waits for them, and re-layouts: 13.3 us -> 6.7 us
    reduce_sum x5 -> x0, other arithmetic: 3.44 us -> none  [the longest x1 3.05 us: local(): new_sum = running_sum * decay_factor + jnp.sum(lifted, axis=1)]
  transfers between devices with their start and end apart: 2 -> 0, of which waited for: 1 -> 0; matrix products, arithmetic and copies ran while one was open for 8% -> 0% of each run, Pallas kernels for 0% -> 0%
where the time goes in v1:
time: 102 us; the launch traced here: 101 us
  Pallas kernels  92.9 us (91%)
  local copies, waits for them, and re-layouts  7.41 us (7%)
    pallas_call x1, Pallas kernels, local(): pl.pallas_call(kernel, out_shape=(jax.ShapeDtypeStruct((2, ROWS, 640), BF...  92.9 us
    unnamed x17, local copies, waits for them, and re-layouts  6.7 us

profile of v1, /device:TPU:1, one launch (start us, length us, event | category | flops | bytes accessed | tf_op | source)
XLA Modules:
  0.0 101.0 jit_solution(3501772486952353364)
XLA Ops:
  0.6 0.0 copy-start.4
  0.6 0.7 reshape.20.gain_ref
  1.3 0.0 copy-done.4
  1.4 0.0 copy-start.5
  1.4 0.7 copy-done.5
  2.0 0.0 copy-start.3
  2.0 0.1 copy.11.scales_ref
  2.1 0.6 copy-done.3
  2.7 0.0 copy-start
  2.7 0.9 copy-done
  3.7 0.0 copy-start.1
  3.7 0.9 copy-done.1
  4.6 0.0 copy-start.2
  4.6 0.9 copy-done.2
  5.5 92.9 %attend_planes.1 = (bf16[2,48,640]{2,1,0:T(8,128)(2,1)S(1)}, bf16[2,48,1280]{2,1,0:T(8,128)(2,1)S(1)}, bf16[2,48,2]{2,1,0:T(8,128)(2,1)S(1)}, f32[4,32]{1,0:T(4,128)S(1)}) custom-call(bf16[2,48,1280]{2,1,0:T(8,128)(2,1)S(1)} %copy-done, f32[1,1280]{1,0:T(1,128)S(1)} %reshape.20.gain_ref, f32[1,1280]{1,0:T(1,128)S(1)} %reshape.21.bias_ref, ...), custom_call_target="tpu_custom_call" | custom-call | tf_op jit(solution)/shard_map/attend_planes/pallas_call | solution.py:593
  98.4 0.7 copy.12
  99.1 0.6 copy.16
  99.7 0.7 copy.17
  100.4 0.6 copy.18
  (1 shorter events, 0.0 us)
Async XLA Ops:
  0.6 0.7 copy-start.4
  1.4 0.7 copy-start.5
  2.0 0.7 copy-start.3
  2.7 0.9 copy-start
  3.7 0.9 copy-start.1
  4.6 0.9 copy-start.2

commit v2 on v1

v2 whole, which is shorter than its diff:
```python
import jax
import jax.numpy as jnp
from jax import lax
from jax.experimental import pallas as pl
from jax.experimental.pallas import tpu as pltpu
from jax.sharding import PartitionSpec as P

HEADS = 10
HEAD_DIM = 64
GROUPS = 32
D = 1280
CPG = 40
ROWS = 48
NY = 8
NZ = 4
NX = 4
QROWS = NY * ROWS
UNITS = 3
CHUNK = UNITS * ROWS + 16
WCOLS = 640
CELLS = 122880.0
KEYS = 9 * QROWS
BIG_NEG = -1e30
OFF = (0, 1, -1, 2, -2, 3, -3, 4)
KV_GROUPS = ((0, 1), (1, 2), (3, 2), (5, 3))
MESH = pl.DeviceIdType.MESH
F32 = jnp.float32
BF16 = jnp.bfloat16


def head_of(group, unit):
    return min(UNITS * group + unit, HEADS - 1)


def lane_low(shape):
    return lax.broadcasted_iota(jnp.int32, shape, 1) < HEAD_DIM


def join_halves(low, low_high, high, high_high):
    left = pltpu.roll(low, HEAD_DIM, 1) if low_high else low
    right = high if high_high else pltpu.roll(high, HEAD_DIM, 1)
    return jnp.where(lane_low(left.shape), left, right)


def kernel(
    hid_ref,
    gain_ref,
    bias_ref,
    stale_ref,
    w_ref,
    codes_ref,
    scales_ref,
    att_ref,
    fvals_ref,
    fscales_ref,
    totals_ref,
    hid,
    gain,
    bias,
    stale,
    w_own,
    codes,
    scales,
    in_sem,
    kvs,
    kv,
    kv2,
    xbuf,
    xn,
    st,
    stbuf,
    stsib,
    stz,
    w32,
    wpack,
    w0,
    w80,
    wbuf,
    qbuf,
    mask,
    fsend,
    fhome,
    asend,
    ahome,
    kvy_s,
    kvy_r,
    kvz_s,
    kvz_r,
    kvsib_s,
    kvsib_r,
    x_s,
    x_r,
    sty_s,
    sty_r,
    stsib_s,
    stsib_r,
    stz_s,
    stz_r,
    p0_s,
    p0_r,
    wy_s,
    wy_r,
    wz_s,
    wz_r,
    wx_s,
    wx_r,
    ws_s,
    ws_r,
    f_s,
    f_r,
    a_s,
    a_r,
):
    img = lax.axis_index("img")
    patch = lax.axis_index("patch")
    x = img % NX
    img_base = img - x
    z = patch // (2 * NY)
    y = (patch // 2) % NY
    c = patch % 2

    def dev(y_at=None, z_at=None, c_at=None, x_at=None):
        yy = y if y_at is None else y_at
        zz = z if z_at is None else z_at
        cc = c if c_at is None else c_at
        xx = x if x_at is None else x_at
        return {"img": img_base + xx, "patch": (zz * NY + yy) * 2 + cc}

    sib = dev(c_at=1 - c)
    y_peers = [dev(y_at=(y + k) % NY) for k in range(1, NY)]
    z_peers = [dev(z_at=(z + k) % NZ) for k in range(1, NZ)]
    x_peers = [dev(x_at=(x + k) % NX) for k in range(1, NX)]
    y_twin = y + 1 - 2 * (y % 2)
    diag = dev(y_at=y_twin, c_at=1 - c)
    everyone = y_peers + z_peers + x_peers + [sib, diag]

    barrier = pltpu.get_barrier_semaphore()
    for peer in everyone:
        pl.semaphore_signal(barrier, inc=1, device_id=peer, device_id_type=MESH)

    img_b = y % 2
    active = (y // 2) == x
    four = (y % 2) * 2 + c
    w_core = c == (y // 2) % 2

    pending = []

    def send(src, dst, s_sem, r_sem, peer, when=None):
        copy = pltpu.make_async_remote_copy(
            src_ref=src, dst_ref=dst, send_sem=s_sem, recv_sem=r_sem, device_id=peer, device_id_type=MESH
        )

        def start():
            copy.start()

        def finish():
            copy.wait_send()

        if when is None:
            start()
            pending.append(finish)
        else:
            pl.when(when)(start)
            pending.append(lambda: pl.when(when)(finish))

    def received(dst, s_sem, r_sem):
        pltpu.make_async_remote_copy(
            src_ref=dst, dst_ref=dst, send_sem=s_sem, recv_sem=r_sem, device_id=sib, device_id_type=MESH
        ).wait_recv()

    copies = []
    sources = (codes_ref, w_ref, scales_ref, hid_ref, stale_ref, gain_ref, bias_ref)
    for k, (src, dst) in enumerate(zip(sources, (codes, w_own, scales, hid, stale, gain, bias))):
        copy = pltpu.make_async_copy(src, dst, in_sem.at[k])
        copy.start()
        copies.append(copy)
    copies[1].wait()

    @pl.when(active)
    def _():
        w32[...] = jnp.zeros_like(w32)
        w32[0:20, :] = w_own[...].astype(F32)

        def piece(block, head):
            unit = block * HEADS + head
            return w32[:, (unit // 2) * 128 : (unit // 2) * 128 + 128], unit % 2 == 1

        for g in range(4):
            h = [head_of(g, s) for s in range(UNITS)]
            plan = [((1, h[s]), (2, h[s])) for s in range(UNITS)]
            plan += [((0, h[0]), (0, h[1])), ((0, h[2]), (0, h[2]))]
            for t, (first, second) in enumerate(plan):
                a, a_high = piece(*first)
                b, b_high = piece(*second)
                wpack[g, :, t * 128 : t * 128 + 128] = join_halves(a, a_high, b, b_high).astype(BF16)

    copies[0].wait()
    copies[2].wait()
    eye_row = lax.broadcasted_iota(jnp.int32, (ROWS, ROWS), 0)
    eye_col = lax.broadcasted_iota(jnp.int32, (ROWS, ROWS), 1)
    eye = jnp.where(eye_row == eye_col, 1.0, 0.0).astype(BF16)
    for b in range(2):
        lane16 = lax.broadcasted_iota(jnp.int32, (16, 128), 1)
        sc = lax.dot_general(eye, scales[b], (((1,), (1,)), ((), ())), preferred_element_type=F32)
        tile = jnp.zeros((16, 128), F32)
        for t in range(3):
            for f in range(2):
                col = sc[t * 16 : t * 16 + 16, f : f + 1]
                tile = jnp.where(lane16 == 2 * t + f, col, tile)
        tile = tile.astype(BF16)
        packed = {}
        for h in range(HEADS):
            k_tile = codes[b, :, (h // 2) * 128 : (h // 2) * 128 + 128].astype(F32)
            v_tile = codes[b, :, 640 + (h // 2) * 128 : 640 + (h // 2) * 128 + 128].astype(F32)
            odd = h % 2 == 1
            packed[h] = join_halves(k_tile, odd, v_tile, odd).astype(BF16)
        for g in range(4):
            for s in range(UNITS):
                kvs[2 * g + b, s * ROWS : (s + 1) * ROWS, :] = packed[head_of(g, s)]
            kvs[2 * g + b, UNITS * ROWS : CHUNK, :] = tile

    copies[3].wait()
    copies[4].wait()
    sub = lax.broadcasted_iota(jnp.int32, (GROUPS, D), 0) * CPG
    lane = lax.broadcasted_iota(jnp.int32, (GROUPS, D), 1)
    spread = jnp.where((lane >= sub) & (lane < sub + CPG), 1.0, 0.0).astype(F32)
    col_sums = []
    for b in range(2):
        feats = hid[b].astype(F32)
        col_sums.append(jnp.sum(feats, axis=0, keepdims=True))
        col_sums.append(jnp.sum(feats * feats, axis=0, keepdims=True))
    col_sums = jnp.concatenate(col_sums, axis=0)
    fresh = lax.dot_general(
        col_sums, spread, (((1,), (1,)), ((), ())), precision=lax.Precision.HIGHEST, preferred_element_type=F32
    )
    st[...] = jnp.zeros_like(st)
    st[0:4, 0:GROUPS] = stale[...]
    st[4:8, 0:GROUPS] = fresh
    stbuf[y] = st[...]

    kv[z, c, 0] = kvs[y]
    xbuf[0] = hid[img_b]

    pl.semaphore_wait(barrier, len(everyone))

    for j in range(4):
        peer = dev(y_at=y - y % 2 + j // 2, c_at=j % 2)
        send(wpack.at[j], w0.at[pl.ds(pl.multiple_of(four * 32, 32), 32)], p0_s.at[j], p0_r.at[four], peer, active & (four != j))

    def kv_to_plane(i):
        send(kvs.at[(y - OFF[i]) % NY], kv.at[z, c, i], kvy_s.at[i], kvy_r.at[i], dev(y_at=(y - OFF[i]) % NY))

    for i in range(1, 5):
        kv_to_plane(i)
    for k in range(1, NY):
        send(st, stbuf.at[y], sty_s.at[k], sty_r.at[y], dev(y_at=(y + k) % NY))
    def kv_part(zz, cc, grp):
        first, count = KV_GROUPS[grp]
        return kv.at[zz, cc, pl.ds(first, count)]

    def kv_own(grp):
        first, count = KV_GROUPS[grp]
        for i in range(first, first + count):
            if i > 0:
                received(kv.at[z, c, i], kvy_s.at[i], kvy_r.at[i])
        part = kv_part(z, c, grp)
        for k in range(1, NZ):
            to = (z + k) % NZ
            near = jnp.abs(to - z) < NZ - 1
            send(part, part, kvz_s.at[k, grp], kvz_r.at[z, grp], dev(z_at=to), near)
        send(part, part, kvsib_s.at[z, grp], kvsib_r.at[z, grp], sib)

    z_next = jnp.where(z == 3, 2, z + 1)
    z_other = jnp.where(z == 0, 2, jnp.where(z == 3, 1, z - 1))
    z_far = jnp.where(z < 2, 3, 0)

    def kv_arrive(grp):
        for zz in (z_next, z_other, z_far):
            part = kv_part(zz, c, grp)
            received(part, kvz_s.at[1, grp], kvz_r.at[zz, grp])
            if zz is z_far:
                middle = (z == 1) | (z == 2)
                send(part, part, kvz_s.at[0, grp], kvz_r.at[zz, grp], dev(z_at=3 - z_far), middle)
            send(part, part, kvsib_s.at[zz, grp], kvsib_r.at[zz, grp], sib)

    own_zc = z * 2 + c
    low16 = lane_low((16, 128))

    def widen(zz, cc, grp):
        place = ((zz * 2 + cc - own_zc) % 8 + 1) * QROWS
        first, count = KV_GROUPS[grp]

        def body(slot, carry):
            scale_tile = kv[zz, cc, slot, UNITS * ROWS : CHUNK, :].astype(F32)
            for t in range(3):
                factor = jnp.where(low16, scale_tile[:, 2 * t : 2 * t + 1], scale_tile[:, 2 * t + 1 : 2 * t + 2])
                at = pl.ds(pl.multiple_of(place + slot * ROWS + t * 16, 16), 16)
                for s in range(UNITS):
                    code = kv[zz, cc, slot, s * ROWS + t * 16 : s * ROWS + t * 16 + 16, :].astype(F32)
                    wide = code * factor
                    high = wide.astype(BF16)
                    kv2[s, at, 0:128] = high
                    kv2[s, at, 128:256] = (wide - high.astype(F32)).astype(BF16)
            return carry

        lax.fori_loop(first, first + count, body, 0)

    def widen_far(grp):
        for zz in (z_next, z_other, z_far):
            widen(zz, c, grp)

    def from_sibling(zz, grp):
        received(kv_part(zz, 1 - c, grp), kvsib_s.at[zz, grp], kvsib_r.at[zz, grp])
        widen(zz, 1 - c, grp)

    def from_sibling_far(grp):
        for zz in (z_next, z_other, z_far):
            from_sibling(zz, grp)

    def x_send(src, i, peer, k, when=None):
        send(src, xbuf.at[i], x_s.at[k], x_r.at[i], peer, when)

    def x_wait(i):
        received(xbuf.at[i], x_s.at[i], x_r.at[i])

    def w_block(zz, xx):
        return wbuf.at[pl.ds(pl.multiple_of((zz * 4 + xx) * 80, 80), 80)]

    def w_along_x(zz):
        for k in range(1, NX):
            send(w_block(zz, x), w_block(zz, x), wx_s.at[zz, k], wx_r.at[zz, x], dev(x_at=(x + k) % NX), w_core)

    def w_four(zz):
        return wbuf.at[pl.ds(pl.multiple_of(zz * 320, 320), 320)]

    kv_own(0)

    for i in range(NY):
        lane_q = lax.broadcasted_iota(jnp.int32, (ROWS, QROWS), 1)
        same = (lane_q >= i * ROWS) & (lane_q < (i + 1) * ROWS)
        mask[i * ROWS : (i + 1) * ROWS, 0:QROWS] = jnp.where(same, 0.0, BIG_NEG)
        mask[i * ROWS : (i + 1) * ROWS, QROWS : 2 * QROWS] = jnp.where(same, BIG_NEG, 0.0)
    copies[5].wait()
    copies[6].wait()

    w_rows = pl.ds(pl.multiple_of((z * 4 + x) * 80, 80), 80)
    for j in range(4):

        @pl.when(active & (four != j))
        def _(j=j):
            received(w0.at[pl.ds(j * 32, 32)], p0_s.at[j], p0_r.at[j])

    @pl.when(active)
    def _():
        w0[pl.ds(pl.multiple_of(four * 32, 32), 32), :] = wpack[four]
        row = lax.broadcasted_iota(jnp.int32, (80, 128), 0)
        col = lax.broadcasted_iota(jnp.int32, (80, 128), 1)
        hit = jnp.zeros((80, 128), F32)
        for a in range(4):
            hit = jnp.where((row >= 20 * a) & (row < 20 * a + 20) & (col == row + 12 * a), 1.0, hit)
        w80[...] = jnp.dot(hit.astype(BF16), w0[...], preferred_element_type=F32).astype(BF16)

    for k in range(2):
        plane = 2 * four + k

        @pl.when(active & (plane == y))
        def _():
            wbuf[w_rows, :] = w80[...]

        send(w80, wbuf.at[w_rows], wy_s.at[k], wy_r.at[0], dev(y_at=plane), active & (plane != y))

    for i in range(5, NY):
        kv_to_plane(i)
    kv_own(1)
    for i in range(1, 5):
        dest = (y - OFF[i]) % NY
        x_send(hid.at[dest % 2], i, dev(y_at=dest), i)

    @pl.when(w_core & jnp.logical_not(active & (y // 2 == four)))
    def _():
        received(w_block(z, x), wy_s.at[0], wy_r.at[0])

    for k in range(1, NZ):
        send(w_block(z, x), w_block(z, x), wz_s.at[k], wz_r.at[z], dev(z_at=(z + k) % NZ), w_core)
    w_along_x(z)
    kv_own(2)
    kv_arrive(0)

    for k in range(1, NY):
        yy = (y + k) % NY
        received(stbuf.at[yy], sty_s.at[k], sty_r.at[yy])
    y_sum = stbuf[0]
    for k in range(1, NY):
        y_sum = y_sum + stbuf[k]
    stsib[0] = y_sum
    send(stsib.at[0], stsib.at[1], stsib_s, stsib_r, sib)

    for zz in (z_next, z_other, z_far):

        @pl.when(w_core)
        def _(zz=zz):
            received(w_block(zz, x), wz_s.at[1], wz_r.at[zz])

        w_along_x(zz)
    kv_own(3)

    received(stsib.at[1], stsib_s, stsib_r)
    stz[z] = stsib[0] + stsib[1]
    for k in range(1, NZ):
        send(stz.at[z], stz.at[z], stz_s.at[k], stz_r.at[z], dev(z_at=(z + k) % NZ))

    for i in (1, 2):
        x_wait(i)
        x_send(xbuf.at[i], 4 + i, dev(y_at=(y - 2 * OFF[i]) % NY), 4 + i)
    kv_arrive(1)
    for grp in range(4):
        widen(z, c, grp)
    for i, core in ((3, 0), (4, 1)):
        x_wait(i)
        x_send(xbuf.at[i], 7, dev(y_at=(y - OFF[i]) % NY), 7 + core, c == core)
    kv_arrive(2)
    for grp in range(4):
        from_sibling(z, grp)

    for zz in range(NZ):
        for k in range(1, NX):
            xx = (x + k) % NX

            @pl.when(w_core)
            def _(zz=zz, xx=xx):
                received(w_block(zz, xx), wx_s.at[zz, 1], wx_r.at[zz, xx])

        send(w_four(zz), w_four(zz), ws_s.at[zz], ws_r.at[zz], sib, w_core)
    for grp in range(3):
        widen_far(grp)
        from_sibling_far(grp)
    kv_arrive(3)

    for k in range(1, NZ):
        zz = (z + k) % NZ
        received(stz.at[zz], stz_s.at[k], stz_r.at[zz])
    total = stz[0]
    for k in range(1, NZ):
        total = total + stz[k]
    totals_ref[...] = total[4:8, 0:GROUPS]
    stat_rows = []
    for i in range(NY):
        own = stbuf[(y + OFF[i]) % NY]
        used = total[0:4, 0:GROUPS] - own[0:4, 0:GROUPS] + own[4:8, 0:GROUPS]
        used = jnp.where(img_b == 0, used[0:2], used[2:4])
        mean = used[0:1] / CELLS
        var = used[1:2] / CELLS - mean * mean
        stat_rows += [mean, lax.rsqrt(var + 1e-5)]
    stats = lax.dot_general(
        jnp.concatenate(stat_rows, axis=0),
        spread,
        (((1,), (0,)), ((), ())),
        precision=lax.Precision.HIGHEST,
        preferred_element_type=F32,
    )
    gain_row = gain[...].reshape(1, D)
    bias_row = bias[...].reshape(1, D)
    for i in range(NY):
        if i > 4:
            x_wait(i)
        feats = xbuf[i].astype(F32)
        normed = (feats - stats[2 * i : 2 * i + 1]) * stats[2 * i + 1 : 2 * i + 2]
        xn[i * ROWS : (i + 1) * ROWS, :] = (normed * gain_row + bias_row).astype(BF16)

    for zz in range(NZ):

        @pl.when(jnp.logical_not(w_core))
        def _(zz=zz):
            received(w_four(zz), ws_s.at[zz], ws_r.at[zz])

    fsend[...] = jnp.dot(xn[...], wbuf[:, 0:384], preferred_element_type=F32).astype(BF16).reshape(NY, ROWS, 384)
    for i in range(1, NY):
        home = (y + OFF[i]) % NY
        send(fsend.at[i], fhome.at[y], f_s.at[i], f_r.at[y], dev(y_at=home))
    fhome[y] = fsend[0]
    q_all = jnp.dot(xn[...], wbuf[:, 384:640], preferred_element_type=F32).astype(BF16).astype(F32) * 0.125
    low = lane_low((QROWS, 128))
    for s in range(UNITS):
        part = q_all[:, 0:128] if s < 2 else q_all[:, 128:256]
        if s == 1:
            part = pltpu.roll(part, HEAD_DIM, 1)
        part = jnp.where(low, part, 0.0).astype(BF16)
        qbuf[s, :, 0:128] = part
        qbuf[s, :, 128:256] = part
        kv2[s, 0:QROWS, 0:128] = fsend[:, :, s * 128 : s * 128 + 128].reshape(QROWS, 128)
        kv2[s, 0:QROWS, 128:256] = jnp.zeros((QROWS, 128), BF16)

    widen_far(3)
    from_sibling_far(3)

    jobs = [(s, at, min(2 * QROWS, KEYS - at)) for s in range(UNITS) for at in range(0, KEYS, 2 * QROWS)]

    def scores_of(s, at, size):
        found = lax.dot_general(
            qbuf[s], kv2[s, at : at + size, :], (((1,), (1,)), ((), ())), preferred_element_type=F32
        )
        return found + mask[...] if at == 0 else found

    def go_home(k):
        for i in range(1, NY):
            home = (y + OFF[i]) % NY
            send(asend.at[k, i], ahome.at[k, y], a_s.at[k, i], a_r.at[k, y], dev(y_at=home))
        ahome[k, y] = asend[k, 0]

    upcoming = scores_of(*jobs[0])
    out = []
    for n, (s, at, size) in enumerate(jobs):
        scores = upcoming
        if n + 1 < len(jobs):
            upcoming = scores_of(*jobs[n + 1])
        top = jnp.max(scores, axis=1, keepdims=True)
        if at == 0:
            new = jnp.broadcast_to(top, (QROWS, 128))
        else:
            new = jnp.maximum(old, top)
            decay = jnp.exp(old - new)
        lifted = jnp.exp(scores - jnp.concatenate([new] * (size // 128), axis=1))
        row_sum = lifted[:, 0:128]
        for k in range(1, size // 128):
            row_sum = row_sum + lifted[:, k * 128 : k * 128 + 128]
        mixed = jnp.dot(lifted.astype(BF16), kv2[s, at : at + size, :], preferred_element_type=F32)
        if at > 0:
            row_sum = running * decay + row_sum
            mixed = acc * jnp.concatenate([decay, decay], axis=1) + mixed
        old, running, acc = new, row_sum, mixed
        if at + size == KEYS:
            out.append((acc[:, 0:128] + acc[:, 128:256]) / jnp.sum(running, axis=1, keepdims=True))
            if s == 1:
                asend[0] = join_halves(out[0], True, out[1], True).astype(BF16).reshape(NY, ROWS, 128)
                go_home(0)
    asend[1] = out[2].astype(BF16).reshape(NY, ROWS, 128)
    go_home(1)

    for k in range(1, NY):
        plane = (y + k) % NY
        received(fhome.at[plane], f_s.at[k], f_r.at[plane])
    for b in range(2):
        blocks = []
        for h in range(HEADS):
            g, s = (h // UNITS, h % UNITS)
            blocks.append(fhome[2 * g + b, :, s * 128 : s * 128 + 128].astype(F32))
        magnitudes = []
        for kind in range(2):
            tiles = [join_halves(blocks[2 * m], kind == 1, blocks[2 * m + 1], kind == 1) for m in range(5)]
            top = jnp.abs(tiles[0])
            for tile in tiles[1:]:
                top = jnp.maximum(top, jnp.abs(tile))
            magnitude = jnp.max(top, axis=1, keepdims=True) + 1e-06
            magnitudes.append(magnitude)
            for m in range(5):
                at = kind * 640 + m * 128
                fvals_ref[b, :, at : at + 128] = (tiles[m] / magnitude).astype(BF16)
        both = jnp.concatenate(magnitudes, axis=1).astype(BF16)
        turned = lax.dot_general(both, eye, (((0,), (0,)), ((), ())), preferred_element_type=F32)
        fscales_ref[b] = turned.astype(BF16)

    for part in range(2):
        for k in range(1, NY):
            plane = (y + k) % NY
            received(ahome.at[part, plane], a_s.at[part, k], a_r.at[part, plane])
    for b in range(2):
        pairs = [ahome[0, 2 * g + b].astype(F32) for g in range(4)]
        lasts = [ahome[1, 2 * g + b].astype(F32) for g in range(4)]
        att_ref[b, :, 0:128] = pairs[0].astype(BF16)
        att_ref[b, :, 128:256] = join_halves(lasts[0], True, pairs[1], False).astype(BF16)
        att_ref[b, :, 256:384] = join_halves(pairs[1], True, lasts[1], True).astype(BF16)
        att_ref[b, :, 384:512] = pairs[2].astype(BF16)
        att_ref[b, :, 512:640] = join_halves(lasts[2], True, pairs[3], False).astype(BF16)

    for finish in pending:
        finish()


def write_out(a, b, c, d, a_out, b_out, c_out, d_out, a_mid, b_mid, c_mid, d_mid, sems):
    mids = (a_mid, b_mid, c_mid, d_mid)
    steps = []
    for k, src in enumerate((a, b, c, d)):
        steps.append(pltpu.make_async_copy(src, mids[k], sems.at[k]))
        steps[k].start()
    out = []
    for k, dst in enumerate((a_out, b_out, c_out, d_out)):
        steps[k].wait()
        out.append(pltpu.make_async_copy(mids[k], dst, sems.at[4 + k]))
        out[k].start()
    for copy in out:
        copy.wait()


def local(hidden_in, gn_gain, gn_bias, stale_local, w_qkv, stale_values, stale_scales):
    dma = pltpu.SemaphoreType.DMA
    vmem = pltpu.VMEM
    scratch = [
        vmem((2, ROWS, D), BF16),
        vmem((D,), F32),
        vmem((D,), F32),
        vmem((4, GROUPS), F32),
        vmem((20, 1920), BF16),
        vmem((2, ROWS, D), BF16),
        vmem((2, 2, ROWS), BF16),
        dma((7,)),
        vmem((NY, CHUNK, 128), BF16),
        vmem((NZ, 2, NY, CHUNK, 128), BF16),
        vmem((UNITS, KEYS, 256), BF16),
        vmem((NY, ROWS, D), BF16),
        vmem((QROWS, D), BF16),
        vmem((8, 128), F32),
        vmem((NY, 8, 128), F32),
        vmem((2, 8, 128), F32),
        vmem((NZ, 8, 128), F32),
        vmem((32, 1920), F32),
        vmem((4, 32, WCOLS), BF16),
        vmem((128, WCOLS), BF16),
        vmem((80, WCOLS), BF16),
        vmem((D, WCOLS), BF16),
        vmem((UNITS, QROWS, 256), BF16),
        vmem((QROWS, 2 * QROWS), F32),
        vmem((NY, ROWS, 384), BF16),
        vmem((NY, ROWS, 384), BF16),
        vmem((2, NY, ROWS, 128), BF16),
        vmem((2, NY, ROWS, 128), BF16),
        dma((NY,)),
        dma((NY,)),
        dma((NZ, 4)),
        dma((NZ, 4)),
        dma((NZ, 4)),
        dma((NZ, 4)),
        dma((NY + 1,)),
        dma((NY,)),
        dma((NY,)),
        dma((NY,)),
        dma(()),
        dma(()),
        dma((NZ,)),
        dma((NZ,)),
        dma((4,)),
        dma((4,)),
        dma((2,)),
        dma((1,)),
        dma((NZ,)),
        dma((NZ,)),
        dma((NZ, NX)),
        dma((NZ, NX)),
        dma((NZ,)),
        dma((NZ,)),
        dma((NY,)),
        dma((NY,)),
        dma((2, NY)),
        dma((2, NY)),
    ]
    whole = pl.BlockSpec(memory_space=pltpu.VMEM)
    anywhere = pl.BlockSpec(memory_space=pl.ANY)
    out_shape = (
        jax.ShapeDtypeStruct((2, ROWS, 640), BF16),
        jax.ShapeDtypeStruct((2, ROWS, D), BF16),
        jax.ShapeDtypeStruct((2, 2, ROWS), BF16),
        jax.ShapeDtypeStruct((4, GROUPS), F32),
    )
    results = pl.pallas_call(
        kernel,
        out_shape=out_shape,
        in_specs=[anywhere] * 7,
        out_specs=(whole,) * 4,
        scratch_shapes=scratch,
        compiler_params=pltpu.CompilerParams(
            collective_id=0, has_side_effects=True, vmem_limit_bytes=56 * 2**20
        ),
        name="attend_planes",
    )(
        hidden_in,
        gn_gain,
        gn_bias,
        stale_local.reshape(4, GROUPS),
        w_qkv,
        stale_values,
        jnp.transpose(stale_scales, (0, 2, 1)),
    )
    attended, fresh_values, fresh_scales, totals = pl.pallas_call(
        write_out,
        out_shape=out_shape,
        in_specs=[anywhere] * 4,
        out_specs=(anywhere,) * 4,
        scratch_shapes=[vmem(o.shape, o.dtype) for o in out_shape] + [dma((8,))],
        compiler_params=pltpu.CompilerParams(vmem_limit_bytes=62 * 2**20),
        name="write_out",
    )(*results)
    return attended, fresh_values, jnp.transpose(fresh_scales, (0, 2, 1)), totals.reshape(2, 2, GROUPS)


def solution(mesh):
    in_specs = (
        P("img", "patch", None),
        P(),
        P(),
        P("img", "patch", None, None),
        P("patch", None),
        P("img", "patch", None),
        P("img", "patch", None),
    )
    out_specs = (
        P("img", "patch", None),
        P("img", "patch", None),
        P("img", "patch", None),
        P("img", None, None),
    )
    return jax.shard_map(local, mesh=mesh, in_specs=in_specs, out_specs=out_specs, check_vma=False)
```

time: 102 us -> 71.6 us (0.70)
  Pallas kernels: 92.9 us -> 70.1 us
  local copies, waits for them, and re-layouts: 7.41 us -> 0 us
    pallas_call x1 -> x2, Pallas kernels: 92.9 us -> 70.1 us  [the longest x1 68.4 us: local(): pl.pallas_call(kernel, out_shape=out_shape, in_specs=[anywhere] * 7, out_...]
    unnamed x17 -> x0, local copies, waits for them, and re-layouts: 6.7 us -> none
where the time goes in v2:
time: 71.6 us; the launch traced here: 70.8 us
  Pallas kernels  70.1 us (98%)
    pallas_call x1, Pallas kernels, local(): pl.pallas_call(kernel, out_shape=out_shape, in_specs=[anywhere] * 7, out_...  68.4 us
    pallas_call x1, Pallas kernels, local(): pl.pallas_call(write_out, out_shape=out_shape, in_specs=[anywhere] * 4, o...  1.77 us

profile of v2, /device:TPU:1, one launch (start us, length us, event | category | flops | bytes accessed | tf_op | source)
XLA Modules:
  0.0 70.8 jit_solution(2654760653412528896)
XLA Ops:
  0.6 68.4 %attend_planes.1 = (bf16[2,48,640]{2,1,0:T(8,128)(2,1)}, bf16[2,48,1280]{2,1,0:T(8,128)(2,1)}, bf16[2,2,48]{2,1,0:T(2,128)(2,1)}, f32[4,32]{1,0:T(4,128)}) custom-call(bf16[2,48,1280]{2,1,0:T(8,128)(2,1)} %hid_ref.1, f32[1280]{0:T(1024)} %gain_ref.1, f32[1280]{0:T(1024)} %bias_ref.1, f32[4,32]{1,0:T(4,128)} %bitcast.4, bf16[20,1920]{1,0:T(8,128)(2,1)} %w_ref.1, ...), custom_call_target="tpu_custom_call" | custom-call | tf_op jit(solution)/shard_map/attend_planes/pallas_call | solution.py:663
  69.0 1.8 %write_out.1 = (bf16[2,48,640]{2,1,0:T(8,128)(2,1)}, bf16[2,48,1280]{2,1,0:T(8,128)(2,1)}, bf16[2,2,48]{2,1,0:T(2,128)(2,1)}, f32[4,32]{1,0:T(4,128)}) custom-call(bf16[2,48,640]{2,1,0:T(8,128)(2,1)} %get-tuple-element.12.a, bf16[2,48,1280]{2,1,0:T(8,128)(2,1)} %get-tuple-element.13.b, bf16[2,2,48]{2,1,0:T(2,128)(2,1)} %get-tuple-element.14.c, ...), custom_call_target="tpu_custom_call" | custom-call | tf_op jit(solution)/shard_map/write_out/pallas_call | solution.py:682

commit v3 on v2

--- a/solution.py
+++ b/solution.py
@@ -130,9 +130,16 @@
     y_peers = [dev(y_at=(y + k) % NY) for k in range(1, NY)]
     z_peers = [dev(z_at=(z + k) % NZ) for k in range(1, NZ)]
     x_peers = [dev(x_at=(x + k) % NX) for k in range(1, NX)]
+    ring = (img // NX) * NZ + z
+
+    def on_ring(step):
+        at = (ring + step) % (2 * NZ)
+        return {"img": (at // NZ) * NX + x, "patch": ((at % NZ) * NY + y) * 2 + c}
+
+    ring_peers = [on_ring(step) for step in (1, -1, 2, -2)]
     y_twin = y + 1 - 2 * (y % 2)
     diag = dev(y_at=y_twin, c_at=1 - c)
-    everyone = y_peers + z_peers + x_peers + [sib, diag]
+    everyone = y_peers + z_peers + x_peers + ring_peers + [sib, diag]
 
     barrier = pltpu.get_barrier_semaphore()
     for peer in everyone:
@@ -369,22 +376,7 @@
 
         send(w80, wbuf.at[w_rows], wy_s.at[k], wy_r.at[0], dev(y_at=plane), active & (plane != y))
 
-    for i in range(5, NY):
-        kv_to_plane(i)
     kv_own(1)
-    for i in range(1, 5):
-        dest = (y - OFF[i]) % NY
-        x_send(hid.at[dest % 2], i, dev(y_at=dest), i)
-
-    @pl.when(w_core & jnp.logical_not(active & (y // 2 == four)))
-    def _():
-        received(w_block(z, x), wy_s.at[0], wy_r.at[0])
-
-    for k in range(1, NZ):
-        send(w_block(z, x), w_block(z, x), wz_s.at[k], wz_r.at[z], dev(z_at=(z + k) % NZ), w_core)
-    w_along_x(z)
-    kv_own(2)
-    kv_arrive(0)
 
     for k in range(1, NY):
         yy = (y + k) % NY
@@ -395,13 +387,42 @@
     stsib[0] = y_sum
     send(stsib.at[0], stsib.at[1], stsib_s, stsib_r, sib)
 
-    for zz in (z_next, z_other, z_far):
+
+    @pl.when(w_core & jnp.logical_not(active & (y // 2 == four)))
+    def _():
+        received(w_block(z, x), wy_s.at[0], wy_r.at[0])
+
+    def w_rows_of(zz, first, count):
+        return wbuf.at[pl.ds(pl.multiple_of((zz * 4 + x) * 80 + first, 16), count)]
+
+    ring_parts = ((1, 0, 80), (-1, 0, 80), (2, 0, 48), (-2, 48, 32))
+    for n, (step, first, count) in enumerate(ring_parts):
+        mine = w_rows_of(z, first, count)
+        send(mine, mine, wz_s.at[n], wz_r.at[n], on_ring(step), w_core)
+    w_along_x(z)
+
+    for i in range(5, NY):
+        kv_to_plane(i)
+
+    kv_own(2)
+
+    for i in range(1, 5):
+        dest = (y - OFF[i]) % NY
+        x_send(hid.at[dest % 2], i, dev(y_at=dest), i)
+
+
+    kv_arrive(0)
+
+    for n, (step, first, count) in enumerate(ring_parts):
+        zz = (z - step) % NZ
 
         @pl.when(w_core)
-        def _(zz=zz):
-            received(w_block(zz, x), wz_s.at[1], wz_r.at[zz])
-
-        w_along_x(zz)
+        def _(n=n, zz=zz, first=first, count=count):
+            received(w_rows_of(zz, first, count), wz_s.at[n], wz_r.at[n])
+
+        if n != 2:
+            w_along_x(zz)
+
     kv_own(3)
 
     received(stsib.at[1], stsib_s, stsib_r)
@@ -409,15 +430,20 @@
     for k in range(1, NZ):
         send(stz.at[z], stz.at[z], stz_s.at[k], stz_r.at[z], dev(z_at=(z + k) % NZ))
 
+
     for i in (1, 2):
         x_wait(i)
         x_send(xbuf.at[i], 4 + i, dev(y_at=(y - 2 * OFF[i]) % NY), 4 + i)
+
     kv_arrive(1)
+
     for grp in range(4):
         widen(z, c, grp)
+
     for i, core in ((3, 0), (4, 1)):
         x_wait(i)
         x_send(xbuf.at[i], 7, dev(y_at=(y - OFF[i]) % NY), 7 + core, c == core)
+
     kv_arrive(2)
     for grp in range(4):
         from_sibling(z, grp)

time: 71.6 us -> 69.8 us (0.975)
  Pallas kernels: 70.1 us -> 69 us
    pallas_call x1, Pallas kernels: 68.4 us -> 67.3 us  [local(): pl.pallas_call(kernel, out_shape=out_shape, in_specs=[anywhere] * 7, out_...]
where the time goes in v3:
time: 69.8 us; the launch traced here: 69.7 us
  Pallas kernels  69 us (99%)
    pallas_call x1, Pallas kernels, local(): pl.pallas_call(kernel, out_shape=out_shape, in_specs=[anywhere] * 7, out_...  67.3 us
    pallas_call x1, Pallas kernels, local(): pl.pallas_call(write_out, out_shape=out_shape, in_specs=[anywhere] * 4, o...  1.77 us

profile of v3, /device:TPU:1, one launch (start us, length us, event | category | flops | bytes accessed | tf_op | source)
XLA Modules:
  0.0 69.7 jit_solution(5941509777531508680)
XLA Ops:
  0.6 67.3 %attend_planes.1 = (bf16[2,48,640]{2,1,0:T(8,128)(2,1)}, bf16[2,48,1280]{2,1,0:T(8,128)(2,1)}, bf16[2,2,48]{2,1,0:T(2,128)(2,1)}, f32[4,32]{1,0:T(4,128)}) custom-call(bf16[2,48,1280]{2,1,0:T(8,128)(2,1)} %hid_ref.1, f32[1280]{0:T(1024)} %gain_ref.1, f32[1280]{0:T(1024)} %bias_ref.1, f32[4,32]{1,0:T(4,128)} %bitcast.4, bf16[20,1920]{1,0:T(8,128)(2,1)} %w_ref.1, ...), custom_call_target="tpu_custom_call" | custom-call | tf_op jit(solution)/shard_map/attend_planes/pallas_call | solution.py:689
  67.9 1.8 %write_out.1 = (bf16[2,48,640]{2,1,0:T(8,128)(2,1)}, bf16[2,48,1280]{2,1,0:T(8,128)(2,1)}, bf16[2,2,48]{2,1,0:T(2,128)(2,1)}, f32[4,32]{1,0:T(4,128)}) custom-call(bf16[2,48,640]{2,1,0:T(8,128)(2,1)} %get-tuple-element.12.a, bf16[2,48,1280]{2,1,0:T(8,128)(2,1)} %get-tuple-element.13.b, bf16[2,2,48]{2,1,0:T(2,128)(2,1)} %get-tuple-element.14.c, ...), custom_call_target="tpu_custom_call" | custom-call | tf_op jit(solution)/shard_map/write_out/pallas_call | solution.py:708

commit v4 on v3

--- a/solution.py
+++ b/solution.py
@@ -448,20 +448,6 @@
     for grp in range(4):
         from_sibling(z, grp)
 
-    for zz in range(NZ):
-        for k in range(1, NX):
-            xx = (x + k) % NX
-
-            @pl.when(w_core)
-            def _(zz=zz, xx=xx):
-                received(w_block(zz, xx), wx_s.at[zz, 1], wx_r.at[zz, xx])
-
-        send(w_four(zz), w_four(zz), ws_s.at[zz], ws_r.at[zz], sib, w_core)
-    for grp in range(3):
-        widen_far(grp)
-        from_sibling_far(grp)
-    kv_arrive(3)
-
     for k in range(1, NZ):
         zz = (z + k) % NZ
         received(stz.at[zz], stz_s.at[k], stz_r.at[zz])
@@ -486,12 +472,32 @@
     )
     gain_row = gain[...].reshape(1, D)
     bias_row = bias[...].reshape(1, D)
-    for i in range(NY):
-        if i > 4:
-            x_wait(i)
+
+    def normalise(i):
         feats = xbuf[i].astype(F32)
         normed = (feats - stats[2 * i : 2 * i + 1]) * stats[2 * i + 1 : 2 * i + 2]
         xn[i * ROWS : (i + 1) * ROWS, :] = (normed * gain_row + bias_row).astype(BF16)
+
+    for i in range(5):
+        normalise(i)
+
+    for zz in range(NZ):
+        for k in range(1, NX):
+            xx = (x + k) % NX
+
+            @pl.when(w_core)
+            def _(zz=zz, xx=xx):
+                received(w_block(zz, xx), wx_s.at[zz, 1], wx_r.at[zz, xx])
+
+        send(w_four(zz), w_four(zz), ws_s.at[zz], ws_r.at[zz], sib, w_core)
+    for grp in range(3):
+        widen_far(grp)
+        from_sibling_far(grp)
+    kv_arrive(3)
+
+    for i in range(5, NY):
+        x_wait(i)
+        normalise(i)
 
     for zz in range(NZ):
 
@@ -528,7 +534,7 @@
         return found + mask[...] if at == 0 else found
 
     def go_home(k):
-        for i in range(1, NY):
+        for i in range(NY - 1, 0, -1):
             home = (y + OFF[i]) % NY
             send(asend.at[k, i], ahome.at[k, y], a_s.at[k, i], a_r.at[k, y], dev(y_at=home))
         ahome[k, y] = asend[k, 0]
@@ -560,7 +566,10 @@
                 asend[0] = join_halves(out[0], True, out[1], True).astype(BF16).reshape(NY, ROWS, 128)
                 go_home(0)
     asend[1] = out[2].astype(BF16).reshape(NY, ROWS, 128)
+    drained = list(pending)
     go_home(1)
+    for finish in drained:
+        finish()
 
     for k in range(1, NY):
         plane = (y + k) % NY
@@ -598,7 +607,7 @@
         att_ref[b, :, 384:512] = pairs[2].astype(BF16)
         att_ref[b, :, 512:640] = join_halves(lasts[2], True, pairs[3], False).astype(BF16)
 
-    for finish in pending:
+    for finish in pending[len(drained) :]:
         finish()
 
 

time: 69.8 us -> 69.3 us (level)
  no operation moved by 1% of the time
where the time goes in v4:
time: 69.3 us; the launch traced here: 69.1 us
  Pallas kernels  68.5 us (99%)
    pallas_call x1, Pallas kernels, local(): pl.pallas_call(kernel, out_shape=out_shape, in_specs=[anywhere] * 7, out_...  66.7 us
    pallas_call x1, Pallas kernels, local(): pl.pallas_call(write_out, out_shape=out_shape, in_specs=[anywhere] * 4, o...  1.77 us

profile of v4, /device:TPU:1, one launch (start us, length us, event | category | flops | bytes accessed | tf_op | source)
XLA Modules:
  0.0 69.1 jit_solution(8024431908303210463)
XLA Ops:
  0.6 66.7 %attend_planes.1 = (bf16[2,48,640]{2,1,0:T(8,128)(2,1)}, bf16[2,48,1280]{2,1,0:T(8,128)(2,1)}, bf16[2,2,48]{2,1,0:T(2,128)(2,1)}, f32[4,32]{1,0:T(4,128)}) custom-call(bf16[2,48,1280]{2,1,0:T(8,128)(2,1)} %hid_ref.1, f32[1280]{0:T(1024)} %gain_ref.1, f32[1280]{0:T(1024)} %bias_ref.1, f32[4,32]{1,0:T(4,128)} %bitcast.4, bf16[20,1920]{1,0:T(8,128)(2,1)} %w_ref.1, ...), custom_call_target="tpu_custom_call" | custom-call | tf_op jit(solution)/shard_map/attend_planes/pallas_call | solution.py:698
  67.4 1.8 %write_out.1 = (bf16[2,48,640]{2,1,0:T(8,128)(2,1)}, bf16[2,48,1280]{2,1,0:T(8,128)(2,1)}, bf16[2,2,48]{2,1,0:T(2,128)(2,1)}, f32[4,32]{1,0:T(4,128)}) custom-call(bf16[2,48,640]{2,1,0:T(8,128)(2,1)} %get-tuple-element.12.a, bf16[2,48,1280]{2,1,0:T(8,128)(2,1)} %get-tuple-element.13.b, bf16[2,2,48]{2,1,0:T(2,128)(2,1)} %get-tuple-element.14.c, ...), custom_call_target="tpu_custom_call" | custom-call | tf_op jit(solution)/shard_map/write_out/pallas_call | solution.py:717
